TPU v7x, 32 devices: a whole 2x2x4 slice. The times are simulated.
32 devices in a mesh: grp: 2 (over y), fsdp: 8 (over z, x), seq: 2 (over core).
Axes of the slice: x: 2, y: 2, z: 4, core: 2. Of those that a mesh axis runs over, the one named last changes fastest.
Arguments:
- image_tokens: bfloat16 [16, 512, 3072], P(('grp', 'fsdp'), 'seq'), parts along dimension 0, may hold values from -6 to 6
- adjoint: bfloat16 [16, 512, 3072], P(('grp', 'fsdp'), 'seq'), parts along dimension 0, may hold values from -24 to 24
- attn_keys: bfloat16 [16, 768, 1536], P(('grp', 'fsdp'), 'seq'), parts along dimension 0, may hold values from -2.5 to 2.5
- attn_values: bfloat16 [16, 768, 1536], P(('grp', 'fsdp'), 'seq'), parts along dimension 0, may hold values from -6 to 6
- w_query: bfloat16 [3072, 1536], P('fsdp', 'seq'), may hold values from -0.109375 to 0.109375
- w_out: bfloat16 [1536, 3072], P('seq', 'fsdp'), may hold values from -0.15625 to 0.15625
- q_gain: float32 [128], replicated, may hold values from 1 to 2.5
- mod_table: float32 [28, 3, 3072], replicated, may hold values from -4 to 4
- timesteps: int32 [16], P(('grp', 'fsdp')), parts along dimension 0, may hold values from 0 to 27
- text_counts: int32 [16], P(('grp', 'fsdp')), parts along dimension 0, may hold values from 1 to 256
Outputs:
- branch_cotangent: float32 [16, 512, 3072], P(('grp', 'fsdp'), 'seq'), parts along dimension 0
There are 2 independent parts, one for each index of `grp`. A program takes and returns all parts, laid end to end along the dimension named above; an argument that names none is the same for every part. Nothing has to cross between parts.
Inputs may be any that keep to these rules, and one draw needn't show every extreme that they name: Of a prompt's 256 text keys, the first text_counts of them are real and the rest are padding.
All inputs are finite; a program needn't handle non-finite values.
Results may differ from a plain program's by a relative error of at most 0.0092.
Values may be sent and summed in bfloat16 or wider, within the bound.
A program may use at most 128 MiB of HBM per device.

v0:
```python
import jax
import jax.numpy as jnp
from jax import lax
from jax.sharding import PartitionSpec as P

HD = 128
TXT_DEV = 128


def contract_last(left, right):
    return lax.dot_general(
        left, right, (((1,), (1,)), ((), ())), preferred_element_type=jnp.float32
    )


def modulate(tokens_in, shift_row, scale_row):
    row_mean = jnp.mean(tokens_in, axis=-1, keepdims=True)
    centred = tokens_in - row_mean
    variance = jnp.mean(centred * centred, axis=-1, keepdims=True)
    return centred * lax.rsqrt(variance + 1e-06) * (1.0 + scale_row) + shift_row


def head_norm(query, gain_vec):
    row_count = query.shape[0]
    grouped = query.reshape(row_count, -1, gain_vec.shape[0])
    square_mean = jnp.mean(grouped * grouped, axis=-1, keepdims=True)
    return (grouped * lax.rsqrt(square_mean + 1e-06) * gain_vec).reshape(row_count, -1)


def attend(q_normed, key_rows, value_rows, grad_out, usable, head_dim):
    row_count = q_normed.shape[0]
    key_count = key_rows.shape[0]
    head_count = q_normed.shape[1] // head_dim
    factor = head_dim ** (-0.5)

    def split_heads(matrix, length):
        return matrix.reshape(length, head_count, head_dim).transpose(1, 0, 2)

    def one_head(pieces):
        query_head, key_head, value_head, grad_head = pieces
        scores = contract_last(query_head, key_head) * factor
        exp_terms = jnp.where(usable[None, :], jnp.exp(scores), 0.0)
        attn_probs = exp_terms / jnp.sum(exp_terms, axis=-1, keepdims=True)
        d_probs = contract_last(grad_head, value_head)
        centre = jnp.sum(attn_probs * d_probs, axis=-1, keepdims=True)
        d_scores = (attn_probs * (d_probs - centre) * factor).astype(jnp.bfloat16)
        return jnp.dot(d_scores, key_head, preferred_element_type=jnp.float32)

    result = lax.map(
        one_head,
        (
            split_heads(q_normed, row_count),
            split_heads(key_rows, key_count),
            split_heads(value_rows, key_count),
            split_heads(grad_out, row_count),
        ),
    )
    return result.transpose(1, 0, 2).reshape(row_count, head_count * head_dim)


def local(
    image_tokens,
    adjoint,
    attn_keys,
    attn_values,
    w_query,
    w_out,
    q_gain,
    mod_table,
    timesteps,
    text_counts,
):
    modulation = lax.dynamic_index_in_dim(mod_table, timesteps[0], 0, keepdims=False)
    shift_row, scale_row, gate_row = (modulation[0], modulation[1], modulation[2])
    tokens_f = image_tokens[0].astype(jnp.float32)
    normed_f, norm_pull = jax.vjp(
        lambda tokens_in: modulate(tokens_in, shift_row, scale_row), tokens_f
    )
    normed = normed_f.astype(jnp.bfloat16)
    d_branch = (gate_row * adjoint[0].astype(jnp.float32)).astype(jnp.bfloat16)
    key_heads, value_heads = (
        lax.all_to_all(attn_keys, "seq", split_axis=2, concat_axis=1, tiled=True),
        lax.all_to_all(attn_values, "seq", split_axis=2, concat_axis=1, tiled=True),
    )
    key_rows = key_heads[0]
    value_rows = value_heads[0]
    positions = jnp.arange(key_rows.shape[0], dtype=jnp.int32)
    usable = (positions >= TXT_DEV * lax.axis_size("seq")) | (positions < text_counts[0])
    query_part, out_part = (
        lax.all_gather(w_query, "seq", axis=1, tiled=True),
        lax.all_gather(w_out, "seq", axis=0, tiled=True),
    )
    query_full, out_full = (
        lax.all_gather(query_part, "fsdp", axis=0, tiled=True),
        lax.all_gather(out_part, "fsdp", axis=1, tiled=True),
    )
    query = jnp.dot(normed, query_full, preferred_element_type=jnp.float32)
    q_normed_f, query_pull = jax.vjp(lambda query_in: head_norm(query_in, q_gain), query)
    q_normed = q_normed_f.astype(jnp.bfloat16)
    d_attn = contract_last(d_branch, out_full).astype(jnp.bfloat16)
    query_heads, grad_heads = (
        lax.all_to_all(q_normed[None], "seq", split_axis=2, concat_axis=1, tiled=True),
        lax.all_to_all(d_attn[None], "seq", split_axis=2, concat_axis=1, tiled=True),
    )
    d_heads = attend(query_heads[0], key_rows, value_rows, grad_heads[0], usable, HD)
    d_qnormed = lax.all_to_all(d_heads[None], "seq", split_axis=1, concat_axis=2, tiled=True)[0]
    d_query = query_pull(d_qnormed)[0].astype(jnp.bfloat16)
    d_normed = contract_last(d_query, query_full)
    return norm_pull(d_normed)[0][None]


def solution(mesh):
    in_specs = (
        P(("grp", "fsdp"), "seq", None),
        P(("grp", "fsdp"), "seq", None),
        P(("grp", "fsdp"), "seq", None),
        P(("grp", "fsdp"), "seq", None),
        P("fsdp", "seq"),
        P("seq", "fsdp"),
        P(),
        P(),
        P(("grp", "fsdp")),
        P(("grp", "fsdp")),
    )
    out_specs = P(("grp", "fsdp"), "seq", None)
    return jax.shard_map(local, mesh=mesh, in_specs=in_specs, out_specs=out_specs, check_vma=False)
```

profile of v0, /device:TPU:0, one launch (start us, length us, event | category | flops | bytes accessed | tf_op | source)
XLA Modules:
  0.0 407.2 jit_solution(502030111424498027)
XLA Ops:
  8.1 12.8 %all-gather.5.cloned.1.call-done = bf16[384,1536]{1,0:T(8,128)(2,1)} async-done(((bf16[384,768]{1,0:T(8,128)(2,1)}), bf16[384,1536]{1,0:T(8,128)(2,1)}) %all-gather.5.cloned.1.call-update) | async-done | bytes 1179664 | tf_op jit(solution)/shard_map/all_gather | solution.py:90
  20.9 11.9 %all-gather.9.cloned.1.call-done = bf16[1536,384]{1,0:T(8,128)(2,1)} async-done(((bf16[768,384]{1,0:T(8,128)(2,1)}), bf16[1536,384]{1,0:T(8,128)(2,1)}) %all-gather.9.cloned.1.call-update) | async-done | bytes 1179664 | tf_op jit(solution)/shard_map/all_gather | solution.py:91
  32.9 3.3 copy.54
  36.7 9.1 %reduce.2 = bf16[1536,384]{1,0:T(8,128)(2,1)S(1)} reduce(bf16[1536,1,384]{2,1,0:T(2,128)(2,1)S(1)} %bitcast.141, bf16[]{:T(256)} %broadcast.105), dimensions={1}, to_apply=%bitcast.100.reduce_sub_computation | reduce | bytes 2359298
  47.0 3.6 all-to-all-start.1
  51.3 6.3 %copy.58 = bf16[1,384,1536]{1,0,2:T(2,128)(2,1)S(1)} copy(bf16[1,384,1536]{2,1,0:T(8,128)(2,1)} %param.15) | data formatting | bytes 2359296 | tf_op args[3]
  57.6 10.1 %reduce.4 = bf16[1536,384]{1,0:T(8,128)(2,1)} reduce(bf16[1536,1,384]{2,1,0:T(2,128)(2,1)S(1)} %bitcast.144, bf16[]{:T(256)} %broadcast.105), dimensions={1}, to_apply=%bitcast.104.reduce_sub_computation | reduce | bytes 2359298
  67.7 2.3 reshape.116
  70.0 4.7 %all-to-all-start.3 = ((bf16[2,2,147456]{2,1,0:T(2,128)(2,1)}), bf16[2,2,147456]{2,1,0:T(2,128)(2,1)}, u32[]{:S(2)}, u32[]{:S(2)}) async-start(bf16[2,2,147456]{2,1,0:T(2,128)(2,1)} %reshape.116), calls=%async_computation.3 | async-start | bytes 2359296 | tf_op jit(solution)/shard_map/all_to_all | solution.py:83
  78.7 2.1 reshape.117
  85.7 88.6 %all-gather.7.cloned.1.call-done = bf16[3072,1536]{1,0:T(8,128)(2,1)} async-done(((bf16[384,1536]{1,0:T(8,128)(2,1)}), bf16[3072,1536]{1,0:T(8,128)(2,1)}) %all-gather.7.cloned.1.call-update) | async-done | bytes 9437200 | tf_op jit(solution)/shard_map/all_gather | solution.py:94
  174.3 12.8 %copy.51 = bf16[1536,3072]{1,0:T(8,128)(2,1)} copy(bf16[1536,3072]{0,1:T(8,128)(2,1)} %bitcast.139) | data formatting | bytes 18874368 | tf_op jit(solution)/shard_map/dot_general | solution.py:97
  187.1 5.5 %multiply_reduce_fusion.2 = (f32[256,12]{0,1:T(8,128)S(1)}, f32[256,12,128]{0,2,1:T(8,128)S(1)}) fusion(bf16[12,128,3072]{2,1,0:T(8,128)(2,1)} %bitcast.140, bf16[1,256,3072]{2,1,0:T(8,128)(2,1)S(1)} %copy-done, f32[3072]{0:T(1024)S(1)} %bitcast.164, f32[3072]{0:T(1024)S(1)} %bitcast.161, f32[256]{0:T(256)S(1)} %fusion.45, f32[256]{0:T(256)S(1)} %broadcast_multiply_fusion), kind=kOutput, calls=%fused_computation.55 | convolution fusion | flops 2421421056 | bytes 12621824 | tf_op jit(solution)/shard_map/dot_general | solution.py:97
  193.1 8.9 %copy.85 = bf16[1,256,1536]{1,0,2:T(2,128)(2,1)S(1)} copy(bf16[1,256,1536]{1,2,0:T(8,128)(2,1)S(1)} %bitcast.154) | data formatting | bytes 1572864 | tf_op jit(solution)/shard_map/convert_element_type | solution.py:99
  202.0 9.1 %reduce.1 = bf16[1536,256]{1,0:T(8,128)(2,1)} reduce(bf16[1536,1,256]{2,1,0:T(2,128)(2,1)S(1)} %bitcast.146, bf16[]{:T(256)} %broadcast.105), dimensions={1}, to_apply=%bitcast.121.reduce_sub_computation | reduce | bytes 1572866
  212.3 5.1 %all_to_all.75 = bf16[2,2,98304]{2,1,0:T(2,128)(2,1)} all-to-all(bf16[2,2,98304]{2,1,0:T(2,128)(2,1)S(1)} %reshape.110), channel_id=1, replica_groups=mesh['grp'=2,'fsdp'=8,'seq'=2] {'seq'}, dimensions={0} | all-to-all | bytes 1572864 | tf_op jit(solution)/shard_map/all_to_all | solution.py:102
  221.5 91.1 %all-gather.11.cloned.1.call-done = bf16[1536,3072]{1,0:T(8,128)(2,1)} async-done(((bf16[1536,384]{1,0:T(8,128)(2,1)}), bf16[1536,3072]{1,0:T(8,128)(2,1)}) %all-gather.11.cloned.1.call-update) | async-done | bytes 9437200 | tf_op jit(solution)/shard_map/all_gather | solution.py:95
  312.6 7.7 %fusion.32 = bf16[1,256,1536]{2,1,0:T(8,128)(2,1)} fusion(bf16[1536,3072]{1,0:T(8,128)(2,1)} %all-gather.11.cloned.1.call-done, bf16[1,256,3072]{2,1,0:T(8,128)(2,1)} %param.13, f32[3072]{0:T(1024)S(1)} %bitcast.163), kind=kOutput, calls=%fused_computation.46 | convolution fusion | flops 2418671616 | bytes 11808768 | tf_op jit(solution)/shard_map/dot_general | solution.py:11
  320.3 3.5 copy.56
  323.8 9.0 %reduce.3 = bf16[1536,256]{1,0:T(8,128)(2,1)} reduce(bf16[1536,1,256]{2,1,0:T(2,128)(2,1)S(1)} %bitcast.145, bf16[]{:T(256)} %broadcast.105), dimensions={1}, to_apply=%bitcast.102.reduce_sub_computation | reduce | bytes 1572866
  334.1 5.1 %all_to_all.76 = bf16[2,2,98304]{2,1,0:T(2,128)(2,1)} all-to-all(bf16[2,2,98304]{2,1,0:T(2,128)(2,1)S(1)} %reshape.114), channel_id=1, replica_groups=mesh['grp'=2,'fsdp'=8,'seq'=2] {'seq'}, dimensions={0} | all-to-all | bytes 1572864 | tf_op jit(solution)/shard_map/all_to_all | solution.py:103
  342.4 34.8 %while.11 = (s32[]{:T(128)}, f32[6,512,128]{1,2,0:T(8,128)}, bf16[6,512,128]{1,2,0:T(8,128)(2,1)}, bf16[6,768,128]{1,2,0:T(8,128)(2,1)}, bf16[6,512,128]{1,2,0:T...) while((s32[]{:T(128)}, f32[6,512,128]{1,2,0:T(8,128)}, ...), condition=%wide.region_6.7_spmd.clone, body=%wide.region_3.6_spmd.clone.sunk | while | flops 306316544 | bytes 8993369 | solution.py:49
  346.0 2.2 fusion.59
  351.8 2.2 fusion.59
  357.6 2.2 fusion.59
  363.4 2.2 fusion.59
  369.2 2.2 fusion.59
  375.0 2.2 fusion.59
  377.2 3.7 copy.65
  380.9 5.0 %all_to_all.77 = f32[1,512,768]{2,0,1:T(1,128)S(1)} all-to-all(f32[1,512,768]{2,0,1:T(1,128)S(1)} %copy.65), channel_id=1, replica_groups=mesh['grp'=2,'fsdp'=8,'seq'=2] {'seq'}, dimensions={1} | all-to-all | bytes 3145728 | tf_op jit(solution)/shard_map/all_to_all | solution.py:106
  391.3 5.6 %fusion.30 = (f32[256]{0:T(256)S(1)}, f32[256,3072]{1,0:T(8,128)S(1)}) fusion(bf16[1,256,3072]{2,1,0:T(8,128)(2,1)S(1)} %copy-done, f32[256]{0:T(256)S(1)} %broadcast_multiply_fusion, f32[3072]{0:T(1024)S(1)} %bitcast.162, bf16[256,1536]{0,1:T(8,128)(2,1)S(1)} %bitcast.160, bf16[3072,1536]{1,0:T(8,128)(2,1)} %all-gather.7.cloned.1.call-done), kind=kOutput, calls=%fused_computation.41 | convolution fusion | flops 2419851008 | bytes 14956544 | tf_op jit(solution)/shard_map/dot_general | solution.py:11
  397.9 2.8 add_bitcast_fusion
  (73 shorter events, 50.3 us)
Async XLA Ops:
  6.5 14.3 %all-gather.5.cloned.1.call-start = ((), (), s32[]{:S(2)}) async-start(), calls=%async_computation.5 | async-start | bytes 1769472 | tf_op jit(solution)/shard_map/all_gather | solution.py:90
  7.3 25.6 %copy-start.3 = (bf16[1,384,1536]{2,1,0:T(8,128)(2,1)S(1)}, bf16[1,384,1536]{2,1,0:T(8,128)(2,1)}, u32[]{:S(2)}) copy-start(bf16[1,384,1536]{2,1,0:T(8,128)(2,1)} %param.14) | copy-start | bytes 3538948
  7.3 25.6 %all-gather.9.cloned.1.call-start = ((), (), s32[]{:S(2)}) async-start(), calls=%async_computation.7 | async-start | bytes 1769472 | tf_op jit(solution)/shard_map/all_gather | solution.py:91
  8.0 166.3 %all-gather.7.cloned.1.call-start = ((), (), s32[]{:S(2)}) async-start(), calls=%async_computation.6 | async-start | bytes 10616832 | tf_op jit(solution)/shard_map/all_gather | solution.py:94
  20.9 291.7 %all-gather.11.cloned.1.call-start = ((), (), s32[]{:S(2)}) async-start(), calls=%async_computation.8 | async-start | bytes 10616832 | tf_op jit(solution)/shard_map/all_gather | solution.py:95
  47.0 22.9 %all-to-all-start.1 = ((bf16[2,2,147456]{2,1,0:T(2,128)(2,1)}), bf16[2,2,147456]{2,1,0:T(2,128)(2,1)S(1)}, u32[]{:S(2)}, u32[]{:S(2)}) async-start(bf16[2,2,147456]{2,1,0:T(2,128)(2,1)} %reshape.112), calls=%async_computation.1 | async-start | bytes 2359296 | tf_op jit(solution)/shard_map/all_to_all | solution.py:82
  70.0 8.7 %all-to-all-start.3 = ((bf16[2,2,147456]{2,1,0:T(2,128)(2,1)}), bf16[2,2,147456]{2,1,0:T(2,128)(2,1)}, u32[]{:S(2)}, u32[]{:S(2)}) async-start(bf16[2,2,147456]{2,1,0:T(2,128)(2,1)} %reshape.116), calls=%async_computation.3 | async-start | bytes 2359296 | tf_op jit(solution)/shard_map/all_to_all | solution.py:83
  82.2 1.6 copy-start
  187.1 5.6 %copy-start.4 = (f32[128]{0:T(128)S(1)}, f32[128]{0:T(128)}, u32[]{:S(2)}) copy-start(f32[128]{0:T(128)} %param.18) | copy-start | bytes 1540
  192.7 9.3 %copy-start.1 = (f32[256,12,128]{0,2,1:T(8,128)}, f32[256,12,128]{0,2,1:T(8,128)S(1)}, u32[]{:S(2)}) copy-start(f32[256,12,128]{0,2,1:T(8,128)S(1)} %get-tuple-element.110) | copy-start | bytes 4718596
  389.0 1.9 copy-start.2
Sparse Core Ops, SparseCore 0:
  8.9 11.9 all-gather.4
  22.4 10.3 all-gather.8
  35.0 139.2 all-gather.6
  176.2 136.3 all-gather.10
where the time goes:
time: 409 us; the launch traced here: 407 us
  waiting for transfers between devices  206 us (50%)
  local copies, waits for them, and re-layouts  64.4 us (16%)
  matrix products  49.7 us (12%)
  other arithmetic  49.5 us (12%)
  blocking collectives  15.3 us (4%)
  between operations  14.1 us (3%)
  starting transfers between devices  8.38 us (2%)
    all_gather x1, waiting for transfers between devices, local(): lax.all_gather(out_part, 'fsdp', axis=1, tiled=True)  91.1 us
    all_gather x1, waiting for transfers between devices, local(): lax.all_gather(query_part, 'fsdp', axis=0, tiled=True)  88.6 us
    unnamed x4, other arithmetic  37.3 us
    dot_general x14, matrix products, contract_last(): lax.dot_general(left, right, (((1,), (1,)), ((), ())), preferred_element_...  31 us
    unnamed x26, local copies, waits for them, and re-layouts  24.5 us
    dot_general x6, matrix products, one_head(): return jnp.dot(d_scores, key_head, preferred_element_type=jnp.float32)  13.2 us
    dot_general x1, local copies, waits for them, and re-layouts, local(): query = jnp.dot(normed, query_full, preferred_element_type=jnp.float32)  12.8 us
    all_gather x1, waiting for transfers between devices, local(): lax.all_gather(w_query, 'seq', axis=1, tiled=True)  12.8 us
  transfers between devices with their start and end apart: 6, of which 4 were waited for; matrix products, arithmetic and copies ran while one was open for 21% of the time, Pallas kernels for 0%

commit v1 on v0

v1 whole, which is shorter than its diff:
```python
import jax
import jax.numpy as jnp
from jax import lax
from jax.sharding import PartitionSpec as P

HD = 128
SWAP = ((0, 1), (1, 0))


def contract_last(left, right):
    return lax.dot_general(
        left, right, (((1,), (1,)), ((), ())), preferred_element_type=jnp.float32
    )


def swap(piece):
    return lax.ppermute(piece, "seq", SWAP)


def local(
    image_tokens,
    adjoint,
    attn_keys,
    attn_values,
    w_query,
    w_out,
    q_gain,
    mod_table,
    timesteps,
    text_counts,
):
    me = lax.axis_index("seq")
    half = w_query.shape[1]
    heads = half // HD
    factor = HD**-0.5
    w_q = lax.all_gather(w_query, "fsdp", axis=0, tiled=True)
    w_o = lax.all_gather(w_out.T, "fsdp", axis=0, tiled=True)

    modulation = lax.dynamic_index_in_dim(mod_table, timesteps[0], 0, keepdims=False)
    shift_row, scale_row, gate_row = (modulation[0], modulation[1], modulation[2])
    tokens = image_tokens[0].astype(jnp.float32)
    mean = jnp.mean(tokens, axis=-1, keepdims=True)
    centred = tokens - mean
    inv = lax.rsqrt(jnp.mean(centred * centred, axis=-1, keepdims=True) + 1e-06)
    normed = (centred * inv * (1.0 + scale_row) + shift_row).astype(jnp.bfloat16)
    d_branch = (gate_row * adjoint[0].astype(jnp.float32)).astype(jnp.bfloat16)

    def halves(rows):
        own = lax.dynamic_slice_in_dim(rows, me * half, half, 1)
        other = lax.dynamic_slice_in_dim(rows, (1 - me) * half, half, 1)
        return jnp.concatenate([own, swap(other)], axis=0)

    keys, values = halves(attn_keys[0]), halves(attn_values[0])
    key_rows = attn_keys.shape[1]
    txt = keys.shape[0] // 3
    spots = jnp.arange(key_rows, dtype=jnp.int32)
    positions = jnp.concatenate([me * key_rows + spots, (1 - me) * key_rows + spots])
    usable = (positions >= txt) | (positions < text_counts[0])

    normed_all = jnp.concatenate([normed, swap(normed)], axis=0)
    d_branch_all = jnp.concatenate([d_branch, swap(d_branch)], axis=0)
    query = jnp.dot(normed_all, w_q, preferred_element_type=jnp.float32)
    d_attn = jnp.dot(d_branch_all, w_o, preferred_element_type=jnp.float32).astype(jnp.bfloat16)
    parts = []
    for head in range(heads):
        cols = slice(head * HD, (head + 1) * HD)
        q_head, k_head, v_head = query[:, cols], keys[:, cols], values[:, cols]
        root = lax.rsqrt(jnp.mean(q_head * q_head, axis=-1, keepdims=True) + 1e-06)
        unit = q_head * root
        q_normed = (unit * q_gain).astype(jnp.bfloat16)
        scores = contract_last(q_normed, k_head) * factor
        terms = jnp.where(usable[None, :], jnp.exp(scores), 0.0)
        probs = terms / jnp.sum(terms, axis=-1, keepdims=True)
        d_probs = contract_last(d_attn[:, cols], v_head)
        centre = jnp.sum(probs * d_probs, axis=-1, keepdims=True)
        d_scores = (probs * (d_probs - centre) * factor).astype(jnp.bfloat16)
        d_unit = jnp.dot(d_scores, k_head, preferred_element_type=jnp.float32) * q_gain
        d_query = root * (d_unit - unit * jnp.mean(d_unit * unit, axis=-1, keepdims=True))
        parts.append(d_query.astype(jnp.bfloat16))
    d_query = jnp.concatenate(parts, axis=1)
    count = tokens.shape[0]
    theirs = contract_last(d_query[count:], w_q).astype(jnp.bfloat16)
    mine = contract_last(d_query[:count], w_q)
    d_normed = mine + swap(theirs).astype(jnp.float32)
    d_hat = d_normed * (1.0 + scale_row)
    hat = centred * inv
    d_mean = jnp.mean(d_hat, axis=-1, keepdims=True)
    d_proj = jnp.mean(d_hat * hat, axis=-1, keepdims=True)
    return (inv * (d_hat - d_mean - hat * d_proj))[None]


def solution(mesh):
    in_specs = (
        P(("grp", "fsdp"), "seq", None),
        P(("grp", "fsdp"), "seq", None),
        P(("grp", "fsdp"), "seq", None),
        P(("grp", "fsdp"), "seq", None),
        P("fsdp", "seq"),
        P("seq", "fsdp"),
        P(),
        P(),
        P(("grp", "fsdp")),
        P(("grp", "fsdp")),
    )
    out_specs = P(("grp", "fsdp"), "seq", None)
    return jax.shard_map(local, mesh=mesh, in_specs=in_specs, out_specs=out_specs, check_vma=False)
```

time: 409 us -> 215 us (0.53)
  waiting for transfers between devices: 206 us -> 139 us
  local copies, waits for them, and re-layouts: 64.4 us -> 6.78 us
  other arithmetic: 49.5 us -> 11.8 us
  blocking collectives: 15.3 us -> 0 us
  matrix products: 49.7 us -> 40.9 us
  starting transfers between devices: 8.38 us -> 1.13 us
    all_gather x4 -> x2, waiting for transfers between devices: 204 us -> 134 us  [the longest x1 72.7 us: local(): w_q = lax.all_gather(w_query, 'fsdp', axis=0, tiled=True)]
    unnamed x4 -> x6, other arithmetic: 37.3 us -> 1.22 us
    unnamed x26 -> x76, local copies, waits for them, and re-layouts: 24.5 us -> 5.01 us
    all_to_all x3 -> x0, blocking collectives: 15.3 us -> none  [the longest x1 5.14 us: local(): lax.all_to_all(d_attn[None], 'seq', split_axis=2, concat_axis=1, tiled=True)]
    dot_general x1 -> x0, local copies, waits for them, and re-layouts: 12.8 us -> none  [local(): query = jnp.dot(normed, query_full, preferred_element_type=jnp.float32)]
    convert_element_type x1 -> x0, local copies, waits for them, and re-layouts: 8.85 us -> none  [local(): q_normed = q_normed_f.astype(jnp.bfloat16)]
    another operation x5 -> x0, local copies, waits for them, and re-layouts: 8.79 us -> none  [the longest x4 5.09 us: split_heads(): return matrix.reshape(length, head_count, head_dim).transpose(1, 0, 2)]
    all_to_all x2 -> x0, starting transfers between devices: 8.27 us -> none  [the longest x1 4.66 us: local(): lax.all_to_all(attn_values, 'seq', split_axis=2, concat_axis=1, tiled=True)]
  transfers between devices with their start and end apart: 6 -> 7, of which waited for: 4 -> 3; matrix products, arithmetic and copies ran while one was open for 21% -> 16% of each run, Pallas kernels for 0% -> 0%
where the time goes in v1:
time: 215 us
  waiting for transfers between devices  139 us (65%)
  matrix products  40.9 us (19%)
  between operations  15.3 us (7%)
  other arithmetic  11.8 us (5%)
  local copies, waits for them, and re-layouts  6.78 us (3%)
    all_gather x1, waiting for transfers between devices, local(): w_q = lax.all_gather(w_query, 'fsdp', axis=0, tiled=True)  72.7 us
    all_gather x1, waiting for transfers between devices, local(): w_o = lax.all_gather(w_out.T, 'fsdp', axis=0, tiled=True)  61.2 us
    dot_general x14, matrix products, contract_last(): lax.dot_general(left, right, (((1,), (1,)), ((), ())), preferred_element_...  25.1 us
    dot_general x1, matrix products, local(): jnp.dot(d_branch_all, w_o, preferred_element_type=jnp.float32)  6.04 us
    dot_general x1, matrix products, local(): query = jnp.dot(normed_all, w_q, preferred_element_type=jnp.float32)  5.89 us
    unnamed x76, local copies, waits for them, and re-layouts  5.01 us
  transfers between devices with their start and end apart: 7, of which 3 were waited for; matrix products, arithmetic and copies ran while one was open for 16% of the time, Pallas kernels for 0%

profile of v1, /device:TPU:0, one launch (start us, length us, event | category | flops | bytes accessed | tf_op | source)
XLA Modules:
  0.0 214.6 jit_solution(10942834821170242803)
XLA Ops:
  8.7 1.7 convert_reduce_fusion
  11.0 1.0 constant_dynamic-slice_fusion
  12.0 1.9 fusion.7
  14.4 0.9 dynamic-slice_bitcast_fusion.2
  15.9 0.9 dynamic-slice_bitcast_fusion
  16.8 1.5 fusion.21
  19.5 72.7 %all-gather.3.cloned.1.call-done = bf16[3072,768]{1,0:T(8,128)(2,1)} async-done(((bf16[384,768]{1,0:T(8,128)(2,1)}), bf16[3072,768]{1,0:T(8,128)(2,1)}) %all-gather.3.cloned.1.call-update) | async-done | bytes 4718608 | tf_op jit(solution)/shard_map/all_gather | solution.py:36
  92.2 5.9 %fusion.13 = f32[512,768]{1,0:T(8,128)S(1)} fusion(bf16[3072,768]{1,0:T(8,128)(2,1)} %all-gather.3.cloned.1.call-done, bf16[256,3072]{1,0:T(8,128)(2,1)} %collective-permute-done, bf16[256,3072]{1,0:T(8,128)(2,1)} %fusion.7), kind=kOutput, calls=%fused_computation.16 | convolution fusion | flops 2422210560 | bytes 9437184 | tf_op jit(solution)/shard_map/dot_general | solution.py:62
  98.7 2.2 %fusion.116 = (f32[512]{0:T(512)}, f32[512,768]{1,0:T(8,128)}) fusion(bf16[384,768]{1,0:T(8,128)(2,1)S(1)} %get-tuple-element.20, bf16[384,768]{1,0:T(8,128)(2,1)S(1)} %collective-permute-done.1, f32[512,768]{1,0:T(8,128)S(1)} %fusion.13, f32[512]{0:T(512)S(1)} %get-tuple-element.56, f32[128]{0:T(128)S(1)} %copy-done.23, pred[768]{0:T(1024)(128)(4,1)S(1)} %compare_or_fusion), kind=kOutput, calls=%fused_computation.213 | convolution fusion | flops 102432256 | bytes 3020288 | tf_op jit(solution)/shard_map/dot_general | solution.py:11
  101.0 2.2 %fusion.111 = (f32[512]{0:T(512)}, f32[512,768]{1,0:T(8,128)}) fusion(bf16[384,768]{1,0:T(8,128)(2,1)S(1)} %get-tuple-element.20, bf16[384,768]{1,0:T(8,128)(2,1)S(1)} %collective-permute-done.1, f32[512,768]{1,0:T(8,128)S(1)} %fusion.13, f32[128]{0:T(128)S(1)} %copy-done.23, f32[512]{0:T(512)S(1)} %get-tuple-element.57, pred[768]{0:T(1024)(128)(4,1)S(1)} %compare_or_fusion), kind=kOutput, calls=%fused_computation.208 | convolution fusion | flops 102432256 | bytes 3020288 | tf_op jit(solution)/shard_map/dot_general | solution.py:11
  103.2 2.3 %fusion.114 = (f32[512]{0:T(512)}, f32[512,768]{1,0:T(8,128)}) fusion(bf16[384,768]{1,0:T(8,128)(2,1)S(1)} %get-tuple-element.20, bf16[384,768]{1,0:T(8,128)(2,1)S(1)} %collective-permute-done.1, f32[512,768]{1,0:T(8,128)S(1)} %fusion.13, f32[512]{0:T(512)S(1)} %get-tuple-element.54, f32[128]{0:T(128)S(1)} %copy-done.23, pred[768]{0:T(1024)(128)(4,1)S(1)} %compare_or_fusion), kind=kOutput, calls=%fused_computation.211 | convolution fusion | flops 102432256 | bytes 3020288 | tf_op jit(solution)/shard_map/dot_general | solution.py:11
  105.5 2.2 %fusion.115 = (f32[512]{0:T(512)}, f32[512,768]{1,0:T(8,128)}) fusion(bf16[384,768]{1,0:T(8,128)(2,1)S(1)} %get-tuple-element.20, bf16[384,768]{1,0:T(8,128)(2,1)S(1)} %collective-permute-done.1, f32[512,768]{1,0:T(8,128)S(1)} %fusion.13, f32[512]{0:T(512)S(1)} %get-tuple-element.55, f32[128]{0:T(128)S(1)} %copy-done.23, pred[768]{0:T(1024)(128)(4,1)S(1)} %compare_or_fusion), kind=kOutput, calls=%fused_computation.212 | convolution fusion | flops 102432256 | bytes 3020288 | tf_op jit(solution)/shard_map/dot_general | solution.py:11
  107.7 2.2 %fusion.113 = (f32[512]{0:T(512)}, f32[512,768]{1,0:T(8,128)}) fusion(bf16[384,768]{1,0:T(8,128)(2,1)S(1)} %get-tuple-element.20, bf16[384,768]{1,0:T(8,128)(2,1)S(1)} %collective-permute-done.1, f32[512,768]{1,0:T(8,128)S(1)} %fusion.13, f32[512]{0:T(512)S(1)} %get-tuple-element.53, f32[128]{0:T(128)S(1)} %copy-done.23, pred[768]{0:T(1024)(128)(4,1)S(1)} %compare_or_fusion), kind=kOutput, calls=%fused_computation.210 | convolution fusion | flops 102432256 | bytes 3020288 | tf_op jit(solution)/shard_map/dot_general | solution.py:11
  109.9 2.2 %fusion.112 = (f32[512]{0:T(512)}, f32[512,768]{1,0:T(8,128)}) fusion(bf16[768,128]{1,0:T(8,128)(2,1)S(1)} %pad_maximum_fusion.2, f32[512,768]{1,0:T(8,128)S(1)} %fusion.13, f32[512]{0:T(512)S(1)} %get-tuple-element.52, f32[128]{0:T(128)S(1)} %copy-done.23, pred[768]{0:T(1024)(128)(4,1)S(1)} %compare_or_fusion), kind=kOutput, calls=%fused_computation.209 | convolution fusion | flops 102039040 | bytes 2037248 | tf_op jit(solution)/shard_map/dot_general | solution.py:11
  112.1 61.2 %all-gather.5.cloned.1.call-done = bf16[3072,768]{0,1:T(8,128)(2,1)} async-done(((bf16[384,768]{0,1:T(8,128)(2,1)}), bf16[3072,768]{0,1:T(8,128)(2,1)}) %all-gather.5.cloned.1.call-update) | async-done | bytes 4718608 | tf_op jit(solution)/shard_map/all_gather | solution.py:37
  173.4 6.0 %fusion.22 = bf16[512,768]{1,0:T(8,128)(2,1)S(1)} fusion(bf16[3072,768]{0,1:T(8,128)(2,1)} %all-gather.5.cloned.1.call-done, bf16[256,3072]{1,0:T(8,128)(2,1)} %collective-permute-done.2, bf16[256,3072]{1,0:T(8,128)(2,1)} %fusion.21), kind=kOutput, calls=%fused_computation.65 | convolution fusion | flops 2422603776 | bytes 8650752 | tf_op jit(solution)/shard_map/dot_general | solution.py:63
  179.5 1.4 multiply_reduce_fusion.4
  181.4 0.9 copy-done.8
  182.3 1.4 multiply_reduce_fusion.5
  184.2 0.9 copy-done.6
  185.1 1.4 multiply_reduce_fusion.2
  187.1 0.7 copy-done.5
  187.9 1.4 multiply_reduce_fusion.3
  189.7 0.9 copy-done.4
  190.6 1.5 multiply_reduce_fusion.1
  192.1 1.4 multiply_reduce_fusion
  194.1 0.8 copy-done.2
  195.0 1.2 multiply_reduce_fusion.6
  197.8 1.4 convolution_convert_fusion
  199.3 3.4 %collective-permute-done.4 = bf16[256,3072]{1,0:T(8,128)(2,1)S(1)} collective-permute-done((bf16[256,3072]{1,0:T(8,128)(2,1)S(1)}, bf16[256,3072]{1,0:T(8,128)(2,1)S(1)}, u32[]{:S(2)}, u32[]{:S(2)}) %collective-permute-start.4) | collective-permute-done | bytes 1572896 | tf_op jit(solution)/shard_map/ppermute | solution.py:17
  202.7 2.0 fusion.25
  204.7 3.0 %fusion.11 = f32[1,256,3072]{2,1,0:T(8,128)} fusion(bf16[1,256,3072]{2,1,0:T(8,128)(2,1)S(1)} %copy-done, f32[256]{0:T(256)S(1)} %broadcast_multiply_fusion.6, f32[256]{0:T(256)S(1)} %broadcast_multiply_fusion.7, f32[256]{0:T(256)S(1)} %copy-done.26, f32[256]{0:T(256)S(1)} %copy-done.22, f32[3072]{0:T(1024)S(1)} %bitcast.60, ...), kind=kLoop, calls=%fused_computation.14 | loop fusion | flops 7864320 | bytes 9453568 | tf_op jit(solution)/shard_map/broadcast_in_dim | solution.py:89
  (114 shorter events, 8.6 us)
Async XLA Ops:
  6.5 3.8 %copy-start = (bf16[1,256,3072]{2,1,0:T(8,128)(2,1)S(1)}, bf16[1,256,3072]{2,1,0:T(8,128)(2,1)}, u32[]{:S(2)}) copy-start(bf16[1,256,3072]{2,1,0:T(8,128)(2,1)} %param.10) | copy-start | bytes 4718596
  6.5 85.6 %all-gather.3.cloned.1.call-start = ((), (), s32[]{:S(2)}) async-start(), calls=%async_computation | async-start | bytes 5308416 | tf_op jit(solution)/shard_map/all_gather | solution.py:36
  7.3 166.1 %all-gather.5.cloned.1.call-start = ((), (), s32[]{:S(2)}) async-start(), calls=%async_computation.1 | async-start | bytes 5308416 | tf_op jit(solution)/shard_map/all_gather | solution.py:37
  10.4 3.6 %copy-start.21 = (f32[256]{0:T(256)}, f32[256]{0:T(256)S(1)}, u32[]{:S(2)}) copy-start(f32[256]{0:T(256)S(1)} %broadcast_multiply_fusion.8) | copy-start | bytes 3076
  10.9 3.0 %copy-start.25 = (f32[256]{0:T(256)}, f32[256]{0:T(256)S(1)}, u32[]{:S(2)}) copy-start(f32[256]{0:T(256)S(1)} %add_rsqrt_fusion.6) | copy-start | bytes 3076
  12.0 2.4 %copy-start.9 = (bf16[1,384,1536]{2,1,0:T(8,128)(2,1)S(1)}, bf16[1,384,1536]{2,1,0:T(8,128)(2,1)}, u32[]{:S(2)}) copy-start(bf16[1,384,1536]{2,1,0:T(8,128)(2,1)} %param.12) | copy-start | bytes 3538948
  13.9 5.5 %collective-permute-start = (bf16[256,3072]{1,0:T(8,128)(2,1)}, bf16[256,3072]{1,0:T(8,128)(2,1)}, u32[]{:S(2)}, u32[]{:S(2)}) collective-permute-start(bf16[256,3072]{1,0:T(8,128)(2,1)} %fusion.7), channel_id=1, source_target_pairs={{0,1},{1,0},{2,3},{3,2},{4,5},{5,4},{6,7},{7,6},{8,9},{9,8},{10,11... | collective-permute-start | bytes 4718600 | tf_op jit(solution)/shard_map/ppermute | solution.py:17
  14.4 1.5 copy-start.10
  15.3 1.6 copy-start.3
  15.3 4.2 %collective-permute-start.1 = (bf16[384,768]{1,0:T(8,128)(2,1)}, bf16[384,768]{1,0:T(8,128)(2,1)S(1)}, u32[]{:S(2)}, u32[]{:S(2)}) collective-permute-start(bf16[384,768]{1,0:T(8,128)(2,1)} %get-tuple-element.19), channel_id=1, source_target_pairs={{0,1},{1,0},{2,3},{3,2},{4,5},{5,4},{6,7},{7,6},{8,9},{9,8},{10,11... | collective-permute-start | bytes 1769480 | tf_op jit(solution)/shard_map/ppermute | solution.py:17
  16.8 162.7 %collective-permute-start.3 = (bf16[384,768]{1,0:T(8,128)(2,1)}, bf16[384,768]{1,0:T(8,128)(2,1)}, u32[]{:S(2)}, u32[]{:S(2)}) collective-permute-start(bf16[384,768]{1,0:T(8,128)(2,1)} %get-tuple-element.24), channel_id=1, source_target_pairs={{0,1},{1,0},{2,3},{3,2},{4,5},{5,4},{6,7},{7,6},{8,9},{9,8},{10,11... | collective-permute-start | bytes 1769480 | tf_op jit(solution)/shard_map/ppermute | solution.py:17
  18.3 93.9 %collective-permute-start.2 = (bf16[256,3072]{1,0:T(8,128)(2,1)}, bf16[256,3072]{1,0:T(8,128)(2,1)}, u32[]{:S(2)}, u32[]{:S(2)}) collective-permute-start(bf16[256,3072]{1,0:T(8,128)(2,1)} %fusion.21), channel_id=1, source_target_pairs={{0,1},{1,0},{2,3},{3,2},{4,5},{5,4},{6,7},{7,6},{8,9},{9,8},{10,11... | collective-permute-start | bytes 4718600 | tf_op jit(solution)/shard_map/ppermute | solution.py:17
  98.1 11.8 %copy-start.1 = (f32[512,768]{1,0:T(8,128)}, f32[512,768]{1,0:T(8,128)S(1)}, u32[]{:S(2)}) copy-start(f32[512,768]{1,0:T(8,128)S(1)} %fusion.13) | copy-start | bytes 4718596
  98.6 9.1 %copy-start.11 = (f32[512]{0:T(512)}, f32[512]{0:T(512)S(1)}, u32[]{:S(2)}) copy-start(f32[512]{0:T(512)S(1)} %get-tuple-element.53) | copy-start | bytes 6148
  98.6 11.3 %copy-start.27 = (f32[512]{0:T(512)}, f32[512]{0:T(512)S(1)}, u32[]{:S(2)}) copy-start(f32[512]{0:T(512)S(1)} %get-tuple-element.52) | copy-start | bytes 6148
  98.6 2.3 %copy-start.15 = (f32[512]{0:T(512)}, f32[512]{0:T(512)S(1)}, u32[]{:S(2)}) copy-start(f32[512]{0:T(512)S(1)} %get-tuple-element.56) | copy-start | bytes 6148
  98.6 4.6 %copy-start.17 = (f32[512]{0:T(512)}, f32[512]{0:T(512)S(1)}, u32[]{:S(2)}) copy-start(f32[512]{0:T(512)S(1)} %get-tuple-element.57) | copy-start | bytes 6148
  101.0 4.5 %copy-start.13 = (f32[512]{0:T(512)}, f32[512]{0:T(512)S(1)}, u32[]{:S(2)}) copy-start(f32[512]{0:T(512)S(1)} %get-tuple-element.54) | copy-start | bytes 6148
  101.0 4.5 %copy-start.19 = (f32[512]{0:T(512)}, f32[512]{0:T(512)S(1)}, u32[]{:S(2)}) copy-start(f32[512]{0:T(512)S(1)} %get-tuple-element.55) | copy-start | bytes 6148
  112.1 67.3 %copy-start.32 = (f32[512]{0:T(512)S(1)}, f32[512]{0:T(512)}, u32[]{:S(2)}) copy-start(f32[512]{0:T(512)} %get-tuple-element.46) | copy-start | bytes 6148
  173.4 6.1 %copy-start.7 = (f32[512,768]{1,0:T(8,128)S(1)}, f32[512,768]{1,0:T(8,128)}, u32[]{:S(2)}) copy-start(f32[512,768]{1,0:T(8,128)} %get-tuple-element.47) | copy-start | bytes 4718596
  183.7 1.4 copy-start.6
  186.4 1.4 copy-start.5
  189.2 1.4 copy-start.4
  190.6 1.5 copy-start.34
  190.6 1.5 copy-start.35
  193.5 1.4 copy-start.2
  193.6 4.1 %slice-start = ((s8[4718592]{0:T(1024)(128)(4,1)}), s8[4194304]{0:T(1024)(128)(4,1)S(1)}, s32[]{:S(2)}) async-start(s8[4718592]{0:T(1024)(128)(4,1)} %bitcast.63), calls=%async_computation.2 | async-start | bytes 8388608
  195.0 2.8 %slice-start.1 = ((s8[4718592]{0:T(1024)(128)(4,1)}), s8[524288]{0:T(1024)(128)(4,1)S(1)}, s32[]{:S(2)}) async-start(s8[4718592]{0:T(1024)(128)(4,1)} %bitcast.63), calls=%async_computation.3 | async-start | bytes 1048576
  197.7 4.9 %copy-start.22 = (f32[256]{0:T(256)S(1)}, f32[256]{0:T(256)}, u32[]{:S(2)}) copy-start(f32[256]{0:T(256)} %copy-done.21) | copy-start | bytes 3076
  197.7 4.9 %copy-start.26 = (f32[256]{0:T(256)S(1)}, f32[256]{0:T(256)}, u32[]{:S(2)}) copy-start(f32[256]{0:T(256)} %copy-done.25) | copy-start | bytes 3076
  199.2 3.5 %collective-permute-start.4 = (bf16[256,3072]{1,0:T(8,128)(2,1)S(1)}, bf16[256,3072]{1,0:T(8,128)(2,1)S(1)}, u32[]{:S(2)}, u32[]{:S(2)}) collective-permute-start(bf16[256,3072]{1,0:T(8,128)(2,1)S(1)} %convolution_convert_fusion), channel_id=1, source_target_pairs={{0,1},{1,0},{2,3},{3,2},{4,5},{5,4},{6,7},{7,6},{8,9},{9,8},{10,11... | collective-permute-start | bytes 4718600 | tf_op jit(solution)/shard_map/ppermute | solution.py:17
  (13 other events, 17.5 us)
Sparse Core Ops, SparseCore 0:
  9.5 82.5 all-gather.2
  94.2 79.1 all-gather.4

commit v2 on v1

v2 whole, which is shorter than its diff:
```python
import functools
import jax
import jax.numpy as jnp
from jax import lax
from jax.experimental import pallas as pl
from jax.experimental.pallas import tpu as pltpu
from jax.sharding import PartitionSpec as P

HD = 128
BF, F32 = jnp.bfloat16, jnp.float32
ROWS = 64
MESH = pl.DeviceIdType.MESH


def contract_last(left, right):
    return lax.dot_general(left, right, (((1,), (1,)), ((), ())), preferred_element_type=F32)


def kernel(
    Z, X,
    tok_ref, adj_ref, key_ref, val_ref, wq_ref, wo_ref, mod_ref, mask_ref, gain_ref,
    out_ref,
    wq, wo, normed, branch, keys, values, query, probs, dattn, dquery, theirs, theirs_in, total,
    recv_sem, send_sem, pair_recv, pair_send, tile_recv, tile_send,
):
    F = Z * X
    S, half = wq_ref.shape
    D = tok_ref.shape[1]
    rows, key_rows = tok_ref.shape[0], key_ref.shape[0]
    heads = half // HD
    factor = HD**-0.5
    g, me, c = lax.axis_index("grp"), lax.axis_index("fsdp"), lax.axis_index("seq")
    z, x = me // X, me % X
    near = [
        (z > 0, {"fsdp": me - X}),
        (z < Z - 1, {"fsdp": me + X}),
        (x > 0, {"fsdp": me - 1}),
        (x < X - 1, {"fsdp": me + 1}),
    ]
    twin, pair = {"grp": 1 - g}, {"seq": 1 - c}

    barrier = pltpu.get_barrier_semaphore()
    for ok, dev in near:
        @pl.when(ok)
        def _(dev=dev):
            pl.semaphore_signal(barrier, inc=1, device_id=dev, device_id_type=MESH)
    pl.semaphore_signal(barrier, inc=1, device_id=twin, device_id_type=MESH)
    pl.semaphore_signal(barrier, inc=1, device_id=pair, device_id_type=MESH)
    present = sum(ok.astype(jnp.int32) for ok, _ in near)
    pl.semaphore_wait(barrier, present + 2)

    bufs = (wq, wo)
    mid = half // 2
    big = (mid // 2 + HD - 1) // HD * HD
    small = mid - big
    M = (g * mid, mid)
    T = ((1 - g) * mid, big)
    Q = (g * mid + big, small)
    N = ((1 - g) * mid, mid)
    U = ((1 - g) * mid + big, small)
    sent = []

    def piece(w, f, span):
        start = pl.multiple_of(f * S, 16)
        return bufs[w].at[pl.ds(start, S), pl.ds(pl.multiple_of(span[0], HD), span[1])]

    def copy(w, f, span, kind, way, dev):
        return pltpu.make_async_remote_copy(
            src_ref=piece(w, f, span), dst_ref=piece(w, f, span),
            send_sem=send_sem.at[way, w, f], recv_sem=recv_sem.at[kind, w, f],
            device_id=dev, device_id_type=MESH,
        )

    def send(ok, *spec):
        sent.append((ok, spec))
        @pl.when(ok)
        def _():
            copy(*spec).start()

    def take(ok, w, f, span, kind):
        @pl.when(ok)
        def _():
            copy(w, f, span, kind, 0, twin).wait_recv()

    def to_x(ok, w, f):
        send(ok & near[2][0], w, f, M, 0, 4, near[2][1])
        send(ok & near[3][0], w, f, M, 0, 5, near[3][1])

    def own_start(w):
        for side in (0, 1):
            ok, dev = near[side]
            send(ok, w, me, M, 0, 2 * side, dev)
        to_x(z >= 0, w, me)
        for side in (0, 1):
            ok, dev = near[side]
            send(ok, w, me, T, 1, 2 * side + 1, dev)

    def z_round(w, d):
        for ok, zz, side in ((z >= d, z - d, 1), (z + d < Z, z + d, 0)):
            f = zz * X + x
            go, dev = near[side]
            take(ok, w, f, M, 0)
            send(ok & go, w, f, M, 0, 2 * side, dev)
            to_x(ok, w, f)
            send(ok, w, f, Q, 2, 6, twin)
            take(ok, w, f, T, 1)
            send(ok & go, w, f, T, 1, 2 * side + 1, dev)

    def planes(d):
        return [(z >= 0, z)] if d == 0 else [(z >= d, z - d), (z + d < Z, z + d)]

    def x_round(w, d):
        for okz, zz in planes(d):
            for e in range(1, X):
                for okx, xx, side in ((x >= e, x - e, 3), (x + e < X, x + e, 2)):
                    ok, f = okz & okx, zz * X + xx
                    go, dev = near[side]
                    take(ok, w, f, M, 0)
                    if X > 2:
                        send(ok & go, w, f, M, 0, 2 + side, dev)
                    send(ok, w, f, M, 1, 6, twin)

    def y_wait(w):
        for d in range(Z):
            for okz, zz in planes(d):
                if d:
                    take(okz, w, zz * X + x, U, 2)
                for e in range(1, X):
                    for okx, xx in ((x >= e, x - e), (x + e < X, x + e)):
                        take(okz & okx, w, zz * X + xx, N, 1)

    mine = pl.ds(pl.multiple_of(me * S, 16), S)
    wq[mine, :] = wq_ref[...]
    own_start(0)
    wo[mine, :] = wo_ref[...]
    own_start(1)

    def swap(src, dst, i):
        return pltpu.make_async_remote_copy(
            src_ref=src, dst_ref=dst, send_sem=pair_send.at[i], recv_sem=pair_recv.at[i],
            device_id=pair, device_id_type=MESH,
        )

    own_heads = pl.ds(pl.multiple_of(c * half, HD), half)
    other_heads = pl.ds(pl.multiple_of((1 - c) * half, HD), half)
    swaps = [
        swap(key_ref.at[:, other_heads], keys.at[pl.ds(key_rows, key_rows), :], 0),
        swap(val_ref.at[:, other_heads], values.at[pl.ds(key_rows, key_rows), :], 1),
    ]
    for s in swaps:
        s.start()

    def stats(r):
        tokens = tok_ref[r, :].astype(F32)
        centred = tokens - jnp.mean(tokens, axis=-1, keepdims=True)
        inv = lax.rsqrt(jnp.mean(centred * centred, axis=-1, keepdims=True) + 1e-06)
        return centred, inv

    def block(i, size):
        return pl.ds(pl.multiple_of(i * size, size), size)

    def prepare(i, carry):
        r = block(i, ROWS)
        centred, inv = stats(r)
        normed[r, :] = (centred * inv * (1.0 + mod_ref[1:2, :]) + mod_ref[0:1, :]).astype(BF)
        branch[r, :] = (mod_ref[2:3, :] * adj_ref[r, :].astype(F32)).astype(BF)
        return carry

    lax.fori_loop(0, rows // ROWS, prepare, 0)
    low, high = pl.ds(0, rows), pl.ds(rows, rows)
    swaps += [
        swap(normed.at[low, :], normed.at[high, :], 2),
        swap(branch.at[low, :], branch.at[high, :], 3),
    ]
    swaps[2].start()
    swaps[3].start()
    keys[pl.ds(0, key_rows), :] = key_ref[:, own_heads]
    values[pl.ds(0, key_rows), :] = val_ref[:, own_heads]

    def make_query():
        def step(i, carry):
            n = block(i, 256)
            query[:, n] = jnp.dot(normed[...], wq[:, n], preferred_element_type=F32)
            return carry
        lax.fori_loop(0, half // 256, step, 0)

    def unit_of(r, h):
        q = query[r, h]
        root = lax.rsqrt(jnp.mean(q * q, axis=-1, keepdims=True) + 1e-06)
        return q * root, root

    def soften(first, last):
        def step(i, carry):
            r, h = block(i % 2, rows), block(i // 2, HD)
            unit, _ = unit_of(r, h)
            scores = contract_last((unit * gain_ref[...]).astype(BF), keys[:, h]) * factor
            terms = jnp.where(mask_ref[...] > 0, jnp.exp(scores), 0.0)
            probs[i // 2, r, :] = terms * (1.0 / jnp.sum(terms, axis=-1, keepdims=True))
            return carry
        lax.fori_loop(2 * first, 2 * last, step, 0)

    for d in range(1, Z):
        z_round(0, d)
        x_round(0, d - 1)
    x_round(0, Z - 1)
    z_round(1, 1)
    x_round(1, 0)
    for s in swaps:
        s.wait()
    y_wait(0)
    make_query()
    z_round(1, 2)
    x_round(1, 1)
    soften(0, heads // 2)
    for d in range(3, Z):
        z_round(1, d)
        x_round(1, d - 1)
    soften(heads // 2, heads)
    x_round(1, Z - 1)
    y_wait(1)

    def make_dattn(i, carry):
        n = block(i, 256)
        dattn[:, n] = jnp.dot(branch[...], wo[:, n], preferred_element_type=F32).astype(BF)
        return carry
    lax.fori_loop(0, half // 256, make_dattn, 0)

    def back(i, carry):
        r, h = block(i % 2, rows), block(i // 2, HD)
        p = probs[i // 2, r, :]
        d_probs = contract_last(dattn[r, h], values[:, h])
        centre = jnp.sum(p * d_probs, axis=-1, keepdims=True)
        d_scores = (p * (d_probs - centre) * factor).astype(BF)
        d_unit = jnp.dot(d_scores, keys[:, h], preferred_element_type=F32) * gain_ref[...]
        unit, root = unit_of(r, h)
        inner = jnp.mean(d_unit * unit, axis=-1, keepdims=True)
        dquery[r, h] = (root * (d_unit - unit * inner)).astype(BF)
        return carry
    lax.fori_loop(0, 2 * heads, back, 0)

    wide = 512
    tiles = D // wide

    def tile_copy(i):
        n = block(i, wide)
        return pltpu.make_async_remote_copy(
            src_ref=theirs.at[:, n], dst_ref=theirs_in.at[:, n],
            send_sem=tile_send.at[i], recv_sem=tile_recv.at[i],
            device_id=pair, device_id_type=MESH,
        )

    def give(i, carry):
        n = block(i, wide)
        theirs[:, n] = contract_last(dquery[high, :], wq[n, :]).astype(BF)
        tile_copy(i).start()
        return carry
    lax.fori_loop(0, tiles, give, 0)

    def keep(i, carry):
        n = block(i, wide)
        total[:, n] = contract_last(dquery[low, :], wq[n, :])
        return carry
    lax.fori_loop(0, tiles, keep, 0)

    def settle(i, carry):
        tile_copy(i).wait()
        return carry
    lax.fori_loop(0, tiles, settle, 0)

    def finish(i, carry):
        r = block(i, ROWS)
        centred, inv = stats(r)
        hat = centred * inv
        d_hat = (total[r, :] + theirs_in[r, :].astype(F32)) * (1.0 + mod_ref[1:2, :])
        d_mean = jnp.mean(d_hat, axis=-1, keepdims=True)
        d_proj = jnp.mean(d_hat * hat, axis=-1, keepdims=True)
        out_ref[r, :] = inv * (d_hat - d_mean - hat * d_proj)
        return carry
    lax.fori_loop(0, rows // ROWS, finish, 0)

    for ok, spec in sent:
        @pl.when(ok)
        def _(spec=spec):
            copy(*spec).wait_send()


def local(
    fsdp,
    image_tokens,
    adjoint,
    attn_keys,
    attn_values,
    w_query,
    w_out,
    q_gain,
    mod_table,
    timesteps,
    text_counts,
):
    X = 2 ** ((fsdp.bit_length() - 1) // 3)
    while fsdp % X:
        X -= 1
    c = lax.axis_index("seq")
    _, rows, D = image_tokens.shape
    S, half = w_query.shape
    key_rows = attn_keys.shape[1]
    modulation = lax.dynamic_index_in_dim(mod_table, timesteps[0], 0, keepdims=False)
    spots = jnp.arange(key_rows, dtype=jnp.int32)
    positions = jnp.concatenate([c * key_rows + spots, (1 - c) * key_rows + spots])
    usable = (positions >= 2 * key_rows // 3) | (positions < text_counts[0])
    vmem = pl.BlockSpec(memory_space=pltpu.VMEM)
    heads = half // HD
    out = pl.pallas_call(
        functools.partial(kernel, fsdp // X, X),
        out_shape=jax.ShapeDtypeStruct((rows, D), F32),
        in_specs=[vmem] * 9,
        out_specs=vmem,
        scratch_shapes=[
            pltpu.VMEM((fsdp * S, half), BF),
            pltpu.VMEM((fsdp * S, half), BF),
            pltpu.VMEM((2 * rows, D), BF),
            pltpu.VMEM((2 * rows, D), BF),
            pltpu.VMEM((2 * key_rows, half), BF),
            pltpu.VMEM((2 * key_rows, half), BF),
            pltpu.VMEM((2 * rows, half), F32),
            pltpu.VMEM((heads, 2 * rows, 2 * key_rows), F32),
            pltpu.VMEM((2 * rows, half), BF),
            pltpu.VMEM((2 * rows, half), BF),
            pltpu.VMEM((rows, D), BF),
            pltpu.VMEM((rows, D), BF),
            pltpu.VMEM((rows, D), F32),
            pltpu.SemaphoreType.DMA((3, 2, fsdp)),
            pltpu.SemaphoreType.DMA((7, 2, fsdp)),
            pltpu.SemaphoreType.DMA((4,)),
            pltpu.SemaphoreType.DMA((4,)),
            pltpu.SemaphoreType.DMA((D // 512,)),
            pltpu.SemaphoreType.DMA((D // 512,)),
        ],
        compiler_params=pltpu.CompilerParams(
            collective_id=0, has_side_effects=True, vmem_limit_bytes=58 * 2**20
        ),
    )(
        image_tokens[0], adjoint[0], attn_keys[0], attn_values[0], w_query, w_out.T,
        modulation, usable.astype(F32)[None], q_gain[None],
    )
    return out[None]


def solution(mesh):
    in_specs = (
        P(("grp", "fsdp"), "seq", None),
        P(("grp", "fsdp"), "seq", None),
        P(("grp", "fsdp"), "seq", None),
        P(("grp", "fsdp"), "seq", None),
        P("fsdp", "seq"),
        P("seq", "fsdp"),
        P(),
        P(),
        P(("grp", "fsdp")),
        P(("grp", "fsdp")),
    )
    out_specs = P(("grp", "fsdp"), "seq", None)
    return jax.shard_map(
        functools.partial(local, mesh.shape["fsdp"]),
        mesh=mesh, in_specs=in_specs, out_specs=out_specs, check_vma=False,
    )
```

time: 215 us -> 126 us (0.59)
  waiting for transfers between devices: 139 us -> 0 us
  Pallas kernels: 0 us -> 117 us
  matrix products: 40.9 us -> 0 us
  between operations: 15.3 us -> 1.44 us
  other arithmetic: 11.8 us -> 0.61 us
    all_gather x2 -> x0, waiting for transfers between devices: 134 us -> none  [the longest x1 72.7 us: local(): w_q = lax.all_gather(w_query, 'fsdp', axis=0, tiled=True)]
    pallas_call x0 -> x1, Pallas kernels: none -> 117 us  [local(): pl.pallas_call(functools.partial(kernel, fsdp // X, X), out_shape=jax.Sha...]
    dot_general x22 -> x0, matrix products: 40.9 us -> none  [the longest x14 25.1 us: contract_last(): lax.dot_general(left, right, (((1,), (1,)), ((), ())), preferred_element_...]
    ppermute x5 -> x0, waiting for transfers between devices: 3.41 us -> none  [swap(): return lax.ppermute(piece, 'seq', SWAP)]
    broadcast_in_dim x1 -> x0, other arithmetic: 3.04 us -> none  [local(): return (inv * (d_hat - d_mean - hat * d_proj))[None]]
    convert_element_type x2 -> x1, other arithmetic: 3.38 us -> 0.6 us  [local(): usable.astype(F32)[None]]
    reduce_sum x3 -> x0, other arithmetic: 2.75 us -> none  [the longest x1 1.7 us: local(): mean = jnp.mean(tokens, axis=-1, keepdims=True)]
    unnamed x76 -> x6, local copies, waits for them, and re-layouts: 5.01 us -> 6.65 us
  transfers between devices with their start and end apart: 7 -> 0, of which waited for: 3 -> 0; matrix products, arithmetic and copies ran while one was open for 16% -> 0% of each run, Pallas kernels for 0% -> 0%
where the time goes in v2:
time: 126 us
  Pallas kernels  117 us (93%)
  local copies, waits for them, and re-layouts  6.69 us (5%)
  between operations  1.44 us (1%)
    pallas_call x1, Pallas kernels, local(): pl.pallas_call(functools.partial(kernel, fsdp // X, X), out_shape=jax.Sha...  117 us
    unnamed x6, local copies, waits for them, and re-layouts  6.65 us

profile of v2, /device:TPU:0, one launch (start us, length us, event | category | flops | bytes accessed | tf_op | source)
XLA Modules:
  0.0 126.1 jit_solution(4977310827196960309)
XLA Ops:
  0.0 0.0 copy-start
  1.4 0.6 or_convert_fusion.mask_ref
  2.0 0.0 copy-done
  2.1 0.6 copy.15
  2.7 2.1 %copy.12 = bf16[768,384]{0,1:T(8,128)(2,1)} copy(bf16[768,384]{1,0:T(8,128)(2,1)} %param.15) | data formatting | bytes 1179648 | tf_op args[5]
  4.8 117.4 %shard_map.100 = f32[256,3072]{1,0:T(8,128)} custom-call(bf16[256,3072]{1,0:T(8,128)(2,1)} %bitcast.18, bf16[256,3072]{1,0:T(8,128)(2,1)} %bitcast.19, bf16[384,1536]{1,0:T(8,128)(2,1)} %bitcast.20, bf16[384,1536]{1,0:T(8,128)(2,1)} %bitcast.21, bf16[384,768]{1,0:T(8,128)(2,1)} %wq_ref.1, bf16[384,768]{1,0:T(8,128)(2,1)} %bitcast.17, f32[3,3072]{1,0:T(4,128)} %bitcast.22, ...), custom_call_target="tpu_custom_call" | custom-call | tf_op jit(solution)/shard_map/pallas_call | solution.py:313
  122.3 3.9 %copy.20 = f32[1,256,3072]{2,1,0:T(8,128)} copy(f32[1,256,3072]{2,1,0:T(8,128)} %bitcast.16) | data formatting | bytes 6291456
  (5 shorter events, 0.0 us)
Async XLA Ops:
  0.0 2.0 %copy-start = (f32[28,3,3072]{2,0,1:T(8,128)S(1)}, f32[28,3,3072]{2,0,1:T(8,128)}, u32[]{:S(2)}) copy-start(f32[28,3,3072]{2,0,1:T(8,128)} %param.17) | copy-start | bytes 3096580

commit v3 on v2

--- a/solution.py
+++ b/solution.py
@@ -86,25 +86,36 @@
         send(ok & near[2][0], w, f, M, 0, 4, near[2][1])
         send(ok & near[3][0], w, f, M, 0, 5, near[3][1])
 
-    def own_start(w):
+    def own_m(w):
+        to_x(z >= 0, w, me)
         for side in (0, 1):
             ok, dev = near[side]
             send(ok, w, me, M, 0, 2 * side, dev)
-        to_x(z >= 0, w, me)
+
+    def own_t(w):
         for side in (0, 1):
             ok, dev = near[side]
             send(ok, w, me, T, 1, 2 * side + 1, dev)
 
-    def z_round(w, d):
+    def z_m(w, d):
         for ok, zz, side in ((z >= d, z - d, 1), (z + d < Z, z + d, 0)):
             f = zz * X + x
             go, dev = near[side]
             take(ok, w, f, M, 0)
             send(ok & go, w, f, M, 0, 2 * side, dev)
             to_x(ok, w, f)
-            send(ok, w, f, Q, 2, 6, twin)
+
+    def z_t(w, d):
+        for ok, zz, side in ((z >= d, z - d, 1), (z + d < Z, z + d, 0)):
+            f = zz * X + x
+            go, dev = near[side]
             take(ok, w, f, T, 1)
             send(ok & go, w, f, T, 1, 2 * side + 1, dev)
+
+    def y_q(w):
+        for d in range(1, Z):
+            for ok, zz in planes(d):
+                send(ok, w, zz * X + x, Q, 2, 6, twin)
 
     def planes(d):
         return [(z >= 0, z)] if d == 0 else [(z >= d, z - d), (z + d < Z, z + d)]
@@ -131,9 +142,9 @@
 
     mine = pl.ds(pl.multiple_of(me * S, 16), S)
     wq[mine, :] = wq_ref[...]
-    own_start(0)
+    own_m(0)
     wo[mine, :] = wo_ref[...]
-    own_start(1)
+    own_m(1)
 
     def swap(src, dst, i):
         return pltpu.make_async_remote_copy(
@@ -177,66 +188,96 @@
     keys[pl.ds(0, key_rows), :] = key_ref[:, own_heads]
     values[pl.ds(0, key_rows), :] = val_ref[:, own_heads]
 
-    def make_query():
+    def columns(which):
+        return pl.ds(pl.multiple_of(which * mid, HD), mid)
+
+    def make_query(which):
+        n = columns(which)
         def step(i, carry):
-            n = block(i, 256)
-            query[:, n] = jnp.dot(normed[...], wq[:, n], preferred_element_type=F32)
+            r = block(i, rows)
+            query[r, n] = jnp.dot(normed[r, :], wq[:, n], preferred_element_type=F32)
             return carry
-        lax.fori_loop(0, half // 256, step, 0)
+        lax.fori_loop(0, 2, step, 0)
 
     def unit_of(r, h):
         q = query[r, h]
         root = lax.rsqrt(jnp.mean(q * q, axis=-1, keepdims=True) + 1e-06)
         return q * root, root
 
-    def soften(first, last):
+    def soften(which, part):
+        head = which * (heads // 2) + part
         def step(i, carry):
-            r, h = block(i % 2, rows), block(i // 2, HD)
+            r, h = block(i, rows), block(head, HD)
             unit, _ = unit_of(r, h)
             scores = contract_last((unit * gain_ref[...]).astype(BF), keys[:, h]) * factor
             terms = jnp.where(mask_ref[...] > 0, jnp.exp(scores), 0.0)
-            probs[i // 2, r, :] = terms * (1.0 / jnp.sum(terms, axis=-1, keepdims=True))
+            probs[head, r, :] = terms * (1.0 / jnp.sum(terms, axis=-1, keepdims=True))
             return carry
-        lax.fori_loop(2 * first, 2 * last, step, 0)
+        lax.fori_loop(0, 2, step, 0)
+
+    def make_dattn(which):
+        n = columns(which)
+        def step(i, carry):
+            r = block(i, rows)
+            dattn[r, n] = jnp.dot(branch[r, :], wo[:, n], preferred_element_type=F32).astype(BF)
+            return carry
+        lax.fori_loop(0, 2, step, 0)
+
+    def back(which, part):
+        head = which * (heads // 2) + part
+        def step(i, carry):
+            r, h = block(i, rows), block(head, HD)
+            p = probs[head, r, :]
+            d_probs = contract_last(dattn[r, h], values[:, h])
+            centre = jnp.sum(p * d_probs, axis=-1, keepdims=True)
+            d_scores = (p * (d_probs - centre) * factor).astype(BF)
+            d_unit = jnp.dot(d_scores, keys[:, h], preferred_element_type=F32) * gain_ref[...]
+            unit, root = unit_of(r, h)
+            inner = jnp.mean(d_unit * unit, axis=-1, keepdims=True)
+            dquery[r, h] = (root * (d_unit - unit * inner)).astype(BF)
+            return carry
+        lax.fori_loop(0, 2, step, 0)
+
+    early, late = g, 1 - g
+    work = [functools.partial(make_query, early)]
+    work += [functools.partial(soften, early, i) for i in range(heads // 2)]
+    work += [functools.partial(make_dattn, early)]
+    work += [functools.partial(back, early, i) for i in range(heads // 2)]
+
+    def some(n):
+        for _ in range(min(n, len(work))):
+            work.pop(0)()
 
     for d in range(1, Z):
-        z_round(0, d)
+        z_m(0, d)
         x_round(0, d - 1)
+        z_m(1, d)
+        x_round(1, d - 1)
+        if d == max(Z - 2, 1):
+            own_t(0)
+            own_t(1)
     x_round(0, Z - 1)
-    z_round(1, 1)
-    x_round(1, 0)
+    y_q(0)
+    z_t(0, 1)
+    x_round(1, Z - 1)
+    y_q(1)
     for s in swaps:
         s.wait()
+    z_t(1, 1)
+    for d in range(2, Z):
+        some(2)
+        z_t(0, d)
+        some(1)
+        z_t(1, d)
+    some(len(work))
     y_wait(0)
-    make_query()
-    z_round(1, 2)
-    x_round(1, 1)
-    soften(0, heads // 2)
-    for d in range(3, Z):
-        z_round(1, d)
-        x_round(1, d - 1)
-    soften(heads // 2, heads)
-    x_round(1, Z - 1)
+    make_query(late)
+    for i in range(heads // 2):
+        soften(late, i)
     y_wait(1)
-
-    def make_dattn(i, carry):
-        n = block(i, 256)
-        dattn[:, n] = jnp.dot(branch[...], wo[:, n], preferred_element_type=F32).astype(BF)
-        return carry
-    lax.fori_loop(0, half // 256, make_dattn, 0)
-
-    def back(i, carry):
-        r, h = block(i % 2, rows), block(i // 2, HD)
-        p = probs[i // 2, r, :]
-        d_probs = contract_last(dattn[r, h], values[:, h])
-        centre = jnp.sum(p * d_probs, axis=-1, keepdims=True)
-        d_scores = (p * (d_probs - centre) * factor).astype(BF)
-        d_unit = jnp.dot(d_scores, keys[:, h], preferred_element_type=F32) * gain_ref[...]
-        unit, root = unit_of(r, h)
-        inner = jnp.mean(d_unit * unit, axis=-1, keepdims=True)
-        dquery[r, h] = (root * (d_unit - unit * inner)).astype(BF)
-        return carry
-    lax.fori_loop(0, 2 * heads, back, 0)
+    make_dattn(late)
+    for i in range(heads // 2):
+        back(late, i)
 
     wide = 512
     tiles = D // wide

time: 126 us -> 110 us (0.87)
  Pallas kernels: 117 us -> 101 us
    pallas_call x1, Pallas kernels: 117 us -> 101 us  [local(): pl.pallas_call(functools.partial(kernel, fsdp // X, X), out_shape=jax.Sha...]
where the time goes in v3:
time: 110 us
  Pallas kernels  101 us (92%)
  local copies, waits for them, and re-layouts  6.69 us (6%)
  between operations  1.44 us (1%)
    pallas_call x1, Pallas kernels, local(): pl.pallas_call(functools.partial(kernel, fsdp // X, X), out_shape=jax.Sha...  101 us
    unnamed x6, local copies, waits for them, and re-layouts  6.65 us

profile of v3, /device:TPU:0, one launch (start us, length us, event | category | flops | bytes accessed | tf_op | source)
XLA Modules:
  0.0 109.6 jit_solution(6792180814092719300)
XLA Ops:
  0.0 0.0 copy-start
  1.4 0.6 or_convert_fusion.mask_ref
  2.0 0.0 copy-done
  2.1 0.6 copy.15
  2.7 2.1 %copy.12 = bf16[768,384]{0,1:T(8,128)(2,1)} copy(bf16[768,384]{1,0:T(8,128)(2,1)} %param.15) | data formatting | bytes 1179648 | tf_op args[5]
  4.8 100.8 %shard_map.100 = f32[256,3072]{1,0:T(8,128)} custom-call(bf16[256,3072]{1,0:T(8,128)(2,1)} %bitcast.18, bf16[256,3072]{1,0:T(8,128)(2,1)} %bitcast.19, bf16[384,1536]{1,0:T(8,128)(2,1)} %bitcast.20, bf16[384,1536]{1,0:T(8,128)(2,1)} %bitcast.21, bf16[384,768]{1,0:T(8,128)(2,1)} %wq_ref.1, bf16[384,768]{1,0:T(8,128)(2,1)} %bitcast.17, f32[3,3072]{1,0:T(4,128)} %bitcast.22, ...), custom_call_target="tpu_custom_call" | custom-call | tf_op jit(solution)/shard_map/pallas_call | solution.py:354
  105.7 3.9 %copy.20 = f32[1,256,3072]{2,1,0:T(8,128)} copy(f32[1,256,3072]{2,1,0:T(8,128)} %bitcast.16) | data formatting | bytes 6291456
  (5 shorter events, 0.0 us)
Async XLA Ops:
  0.0 2.0 %copy-start = (f32[28,3,3072]{2,0,1:T(8,128)S(1)}, f32[28,3,3072]{2,0,1:T(8,128)}, u32[]{:S(2)}) copy-start(f32[28,3,3072]{2,0,1:T(8,128)} %param.17) | copy-start | bytes 3096580

commit v4 on v3

--- a/solution.py
+++ b/solution.py
@@ -18,15 +18,16 @@
 
 def kernel(
     Z, X,
-    tok_ref, adj_ref, key_ref, val_ref, wq_ref, wo_ref, mod_ref, mask_ref, gain_ref,
+    tok_hbm, adj_hbm, key_ref, val_ref, wq_ref, wo_ref, mod_ref, mask_ref, gain_ref,
     out_ref,
     wq, wo, normed, branch, keys, values, query, probs, dattn, dquery, theirs, theirs_in, total,
+    tok_ref, adj_ref, load_sem,
     recv_sem, send_sem, pair_recv, pair_send, tile_recv, tile_send,
 ):
     F = Z * X
     S, half = wq_ref.shape
-    D = tok_ref.shape[1]
-    rows, key_rows = tok_ref.shape[0], key_ref.shape[0]
+    D = tok_hbm.shape[1]
+    rows, key_rows = tok_hbm.shape[0], key_ref.shape[0]
     heads = half // HD
     factor = HD**-0.5
     g, me, c = lax.axis_index("grp"), lax.axis_index("fsdp"), lax.axis_index("seq")
@@ -143,7 +144,13 @@
     mine = pl.ds(pl.multiple_of(me * S, 16), S)
     wq[mine, :] = wq_ref[...]
     own_m(0)
-    wo[mine, :] = wo_ref[...]
+    loads = [
+        pltpu.make_async_copy(tok_hbm, tok_ref, load_sem.at[0]),
+        pltpu.make_async_copy(adj_hbm, adj_ref, load_sem.at[1]),
+    ]
+    for load in loads:
+        load.start()
+    wo[mine, :] = wo_ref[...].T
     own_m(1)
 
     def swap(src, dst, i):
@@ -177,6 +184,8 @@
         branch[r, :] = (mod_ref[2:3, :] * adj_ref[r, :].astype(F32)).astype(BF)
         return carry
 
+    for load in loads:
+        load.wait()
     lax.fori_loop(0, rows // ROWS, prepare, 0)
     low, high = pl.ds(0, rows), pl.ds(rows, rows)
     swaps += [
@@ -354,7 +363,7 @@
     out = pl.pallas_call(
         functools.partial(kernel, fsdp // X, X),
         out_shape=jax.ShapeDtypeStruct((rows, D), F32),
-        in_specs=[vmem] * 9,
+        in_specs=[pl.BlockSpec(memory_space=pl.ANY)] * 2 + [vmem] * 7,
         out_specs=vmem,
         scratch_shapes=[
             pltpu.VMEM((fsdp * S, half), BF),
@@ -370,6 +379,9 @@
             pltpu.VMEM((rows, D), BF),
             pltpu.VMEM((rows, D), BF),
             pltpu.VMEM((rows, D), F32),
+            pltpu.VMEM((rows, D), BF),
+            pltpu.VMEM((rows, D), BF),
+            pltpu.SemaphoreType.DMA((2,)),
             pltpu.SemaphoreType.DMA((3, 2, fsdp)),
             pltpu.SemaphoreType.DMA((7, 2, fsdp)),
             pltpu.SemaphoreType.DMA((4,)),
@@ -381,7 +393,7 @@
             collective_id=0, has_side_effects=True, vmem_limit_bytes=58 * 2**20
         ),
     )(
-        image_tokens[0], adjoint[0], attn_keys[0], attn_values[0], w_query, w_out.T,
+        image_tokens[0], adjoint[0], attn_keys[0], attn_values[0], w_query, w_out,
         modulation, usable.astype(F32)[None], q_gain[None],
     )
     return out[None]

time: 110 us -> 107 us (0.973)
  local copies, waits for them, and re-layouts: 6.69 us -> 4.57 us
  Pallas kernels: 101 us -> 99.8 us
    unnamed x6 -> x5, local copies, waits for them, and re-layouts: 6.65 us -> 4.53 us
where the time goes in v4:
time: 107 us; the launch traced here: 106 us
  Pallas kernels  99.8 us (93%)
  local copies, waits for them, and re-layouts  4.57 us (4%)
  between operations  1.44 us (1%)
    pallas_call x1, Pallas kernels, local(): pl.pallas_call(functools.partial(kernel, fsdp // X, X), out_shape=jax.Sha...  99.8 us
    unnamed x5, local copies, waits for them, and re-layouts  4.53 us

profile of v4, /device:TPU:0, one launch (start us, length us, event | category | flops | bytes accessed | tf_op | source)
XLA Modules:
  0.0 106.4 jit_solution(3040802637703503255)
XLA Ops:
  0.0 0.0 copy-start
  1.4 0.6 or_convert_fusion.mask_ref
  2.0 0.0 copy-done
  2.1 0.6 copy.13
  2.7 99.8 %shard_map.100 = f32[256,3072]{1,0:T(8,128)} custom-call(bf16[256,3072]{1,0:T(8,128)(2,1)} %bitcast.16, bf16[256,3072]{1,0:T(8,128)(2,1)} %bitcast.17, bf16[384,1536]{1,0:T(8,128)(2,1)} %bitcast.18, bf16[384,1536]{1,0:T(8,128)(2,1)} %bitcast.19, bf16[384,768]{1,0:T(8,128)(2,1)} %wq_ref.1, bf16[768,384]{1,0:T(8,128)(2,1)} %wo_ref.1, f32[3,3072]{1,0:T(4,128)} %bitcast.20, ...), custom_call_target="tpu_custom_call" | custom-call | tf_op jit(solution)/shard_map/pallas_call | solution.py:363
  102.5 3.9 %copy.18 = f32[1,256,3072]{2,1,0:T(8,128)} copy(f32[1,256,3072]{2,1,0:T(8,128)} %bitcast.15) | data formatting | bytes 6291456
  (5 shorter events, 0.0 us)
Async XLA Ops:
  0.0 2.0 %copy-start = (f32[28,3,3072]{2,0,1:T(8,128)S(1)}, f32[28,3,3072]{2,0,1:T(8,128)}, u32[]{:S(2)}) copy-start(f32[28,3,3072]{2,0,1:T(8,128)} %param.17) | copy-start | bytes 3096580
